TPU v7x, 128 devices: a whole 4x4x4 slice. The times are simulated.
128 devices in a mesh: row: 16 (over z, y_lo, core), col: 8 (over y_hi, x).
Axes of the slice: x: 4, y: 4 (y_hi: 2, y_lo: 2; y = y_hi * 2 + y_lo), z: 4, core: 2. Of those that a mesh axis runs over, the one named last changes fastest.
Arguments:
- gram_x: float32 [8192, 8192], P('row', 'col'), may hold values from -0.44194174 to 0.44194174, as said below
- cross: float32 [8192, 8192], P('row', 'col'), may hold values from -0.0625 to 0.0625
- gram_y: float32 [8192, 8192], P('row', 'col'), may hold values from -0.44194174 to 0.44194174, as said below
- shifts: float32 [4], replicated, may hold values from -1.5 to 1.5
- modes: bfloat16 [2048, 8192], P('row', 'col'), may hold values from -6 to 6
Outputs:
- products: float32 [4, 2048, 8192], P(None, 'row', 'col')
Inputs may be any that keep to these rules, and one draw needn't show every extreme that they name: `gram_x`: exactly symmetric. `gram_y`: exactly symmetric.
All inputs are finite; a program needn't handle non-finite values.
Results may differ from a plain program's by a relative error of at most 0.0029.
Values may be sent and summed in bfloat16 or wider, within the bound.
No kernel may reach another device: no remote copies, remote signals or barrier semaphores. Data moves between devices by JAX's collectives and lax.ppermute only.
A program may use at most 192 MiB of HBM per device.

v0:
```python
import jax
import jax.numpy as jnp
from jax import lax
from jax.experimental import pallas as pl
from jax.experimental.pallas import tpu as pltpu
from jax.sharding import PartitionSpec as P

BOTH = ("row", "col")
BF16 = jnp.bfloat16
F32 = jnp.float32
VMEM_BYTES = 48 * 2**20


def moves(n_row, n_col, target):
    pairs = []
    for block in range(n_row // 2):
        for core in range(2):
            for col in range(n_col):
                to_block, to_core, to_col = target(block, core, col)
                pairs.append(((2 * block + core) * n_col + col, (2 * to_block + to_core) * n_col + to_col))
    return pairs


def after(array, *others):
    return lax.optimization_barrier((array,) + others)[0]


def call(body, place, grid, in_specs, out_spec, out_shape, scratch, flops, *args):
    return pl.pallas_call(
        body,
        grid_spec=pltpu.PrefetchScalarGridSpec(
            num_scalar_prefetch=1, grid=grid, in_specs=in_specs, out_specs=out_spec, scratch_shapes=scratch
        ),
        out_shape=out_shape,
        compiler_params=pltpu.CompilerParams(vmem_limit_bytes=VMEM_BYTES),
        cost_estimate=pl.CostEstimate(
            flops=flops,
            bytes_accessed=sum(a.size * a.dtype.itemsize for a in args) + out_shape.size * 2,
            transcendentals=0,
        ),
    )(place, *args)


def untransposed(part, mine, other, place):
    slots, modes, depth = part.shape
    half, width = mine.shape
    block = 512

    def body(place, part, mine, other, out, tile):
        tile[pl.ds(pl.multiple_of(place[0] * half, half), half)] = mine[...].astype(BF16)
        tile[pl.ds(pl.multiple_of((1 - place[0]) * half, half), half)] = other[...].astype(BF16)
        rows = part[...].reshape(slots * modes, depth)
        total = jnp.dot(rows, tile[...], preferred_element_type=F32).astype(BF16)
        for slot in range(slots):
            out[place[1 + slot]] = total[slot * modes : (slot + 1) * modes]

    return call(
        body,
        place,
        (width // block,),
        [
            pl.BlockSpec((slots, modes, depth), lambda n, place: (0, 0, 0)),
            pl.BlockSpec((half, block), lambda n, place: (0, n)),
            pl.BlockSpec((half, block), lambda n, place: (0, n)),
        ],
        pl.BlockSpec((slots, modes, block), lambda n, place: (0, 0, n)),
        jax.ShapeDtypeStruct((slots, modes, width), BF16),
        [pltpu.VMEM((2 * half, block), BF16)],
        2 * slots * modes * depth * width,
        part,
        mine,
        other,
    )


def transposed(part, mine, other, place):
    slots, modes, depth = part.shape
    half = mine.shape[0]
    block = 512
    blocks = half // block

    def body(place, part, mine, other, out):
        own = pl.program_id(0) // blocks == place[0]
        tile = jnp.where(own, mine[...], other[...]).astype(BF16)
        rows = part[...].reshape(slots * modes, depth)
        total = lax.dot_general(rows, tile, (((1,), (1,)), ((), ())), preferred_element_type=F32)
        total = total.astype(BF16)
        for slot in range(slots):
            out[place[1 + slot]] = total[slot * modes : (slot + 1) * modes]

    return call(
        body,
        place,
        (2 * blocks,),
        [
            pl.BlockSpec((slots, modes, depth), lambda n, place: (0, 0, 0)),
            pl.BlockSpec((block, depth), lambda n, place: (n % blocks, 0)),
            pl.BlockSpec((block, depth), lambda n, place: (n % blocks, 0)),
        ],
        pl.BlockSpec((slots, modes, block), lambda n, place: (0, 0, n)),
        jax.ShapeDtypeStruct((slots, modes, 2 * half), BF16),
        [],
        4 * slots * modes * depth * half,
        part,
        mine,
        other,
    )


def shards(n_row, n_col, gram_x, cross, gram_y, shifts, modes):
    row, col = lax.axis_index("row"), lax.axis_index("col")
    core, block = row % 2, row // 2
    n_block = n_row // 2
    ring = n_col // 2
    swap_cores = moves(n_row, n_col, lambda block, core, col: (block, 1 - core, col))

    turned = lax.ppermute(
        modes, BOTH, moves(n_row, n_col, lambda block, core, col: (col, core, block ^ col))
    )
    z_turns = [
        moves(n_row, n_col, lambda block, core, col: ((block + 2 * step) % n_block, core, col)) for step in range(4)
    ]
    z_ring = (z_turns[1], z_turns[3])
    pair = lax.ppermute(modes, BOTH, moves(n_row, n_col, lambda block, core, col: (block ^ 1, core, col)))
    gram_x_pair, cross_pair, gram_y_pair = [
        (tile, lax.ppermute(tile, BOTH, swap_cores)) for tile in (gram_x, cross, gram_y)
    ]
    pair = after(jnp.stack((modes, pair)), gram_x_pair, cross_pair, gram_y_pair)
    before, behind = lax.ppermute(pair, BOTH, z_ring[0]), lax.ppermute(pair, BOTH, z_ring[1])
    across = (lax.ppermute(before[:1], BOTH, z_ring[0]), lax.ppermute(behind[1:], BOTH, z_ring[1]))
    stripe = jnp.concatenate((pair, before, behind) + across, axis=0)

    copies = jnp.broadcast_to(after(turned, pair)[None], (n_col,) + turned.shape)
    swath = lax.all_to_all(copies, "col", split_axis=0, concat_axis=0, tiled=True)

    def start(product, ahead, back):
        parts = product.reshape((4, 2, -1) + product.shape[2:])
        return parts, lax.ppermute(parts[2, 0], BOTH, ahead), lax.ppermute(parts[2, 1], BOTH, back)

    def join(parts, came_ahead, came_back):
        def plus(part, came):
            return (part.astype(F32) + came.astype(F32)).astype(BF16)

        return (
            parts[0],
            jnp.stack((plus(parts[1, 0], came_ahead), parts[1, 1])),
            jnp.stack((parts[3, 0], plus(parts[3, 1], came_back))),
        )

    def finish(parts, ahead, back):
        mine, on, off = parts
        return (
            mine.astype(F32)
            + lax.ppermute(on, BOTH, ahead).astype(F32)
            + lax.ppermute(off, BOTH, back).astype(F32)
        )

    def ring_sum(parts, pairs):
        return parts[0].astype(F32) + sum(lax.ppermute(parts[i], BOTH, pairs[i]).astype(F32) for i in (1, 3, 2))

    def later(parts, *others):
        return lax.optimization_barrier(tuple(parts) + others)[: len(parts)]

    def fold(total, partner, dtype):
        return total[0] + lax.ppermute(total[1].astype(dtype), BOTH, partner).astype(F32)

    x_ring = [
        moves(n_row, n_col, lambda block, core, col: (block, core, col // ring * ring + (col + way) % ring))
        for way in (1, -1)
    ]
    y_near = moves(n_row, n_col, lambda block, core, col: (block ^ 1, core, col))
    y_far = moves(n_row, n_col, lambda block, core, col: (block, core, col ^ ring))

    slots = jnp.arange(n_block)
    owner = slots ^ block
    z_ahead, y_other = (owner // 2 - block // 2) % 4, (owner ^ block) % 2
    here = jnp.concatenate((core[None], 2 * z_ahead + y_other))
    here_y = jnp.concatenate((core[None], 4 * y_other + z_ahead))
    held = ((block + 2 * jnp.array((0, 0, -1, -1, 1, 1, 2, 2))) % n_block) ^ (slots % 2)
    summed = held ^ block
    there = jnp.concatenate((core[None], 2 * ((summed - col) % ring) + (summed // ring ^ col // ring)))

    turned_a = transposed(stripe, *cross_pair, there)
    step_t = start(turned_a, *x_ring)
    product_y = untransposed(after(swath, turned_a), *gram_y_pair, here)
    step_y = start(product_y, *z_ring)
    step_t = join(*later(step_t, product_y))
    product_a = untransposed(after(swath, step_t[1]), *cross_pair, here_y)
    product_a = product_a.reshape((2, 4) + product_a.shape[1:])
    product_x = untransposed(after(swath, product_a), *gram_x_pair, here)
    step_x = start(product_x, *z_ring)
    step_y = join(*later(step_y, product_x))
    total_t = after(finish(step_t, *x_ring), step_y[1])
    step_x = join(*later(step_x, total_t))
    half_a = after(fold(product_a, y_near, BF16).astype(BF16), step_x[1])

    total_t = after(fold(total_t, y_far, BF16), half_a)
    from_gram_y = fold(finish(step_y, *z_ring), y_near, BF16)
    from_gram_x = fold(after(finish(step_x, *z_ring), total_t), y_near, BF16)
    from_cross_t = ring_sum(half_a, z_turns)
    home = lax.ppermute(
        total_t.astype(BF16), BOTH, moves(n_row, n_col, lambda block, core, col: (block ^ col, core, col))
    )
    home = lax.ppermute(home, BOTH, moves(n_row, n_col, lambda block, core, col: (block, core, col ^ block)))
    from_cross = home.astype(F32)

    shift_col = shifts[:, None, None]
    return (
        from_gram_y[None]
        - shift_col * (from_cross_t + from_cross)[None]
        + shift_col * shift_col * from_gram_x[None]
    )


def solution(mesh):
    def step(*args):
        return shards(mesh.shape["row"], mesh.shape["col"], *args)

    in_specs = (P("row", "col"), P("row", "col"), P("row", "col"), P(), P("row", "col"))
    out_specs = P(None, "row", "col")
    return jax.shard_map(step, mesh=mesh, in_specs=in_specs, out_specs=out_specs, check_vma=False)
```

profile of v0, /device:TPU:120, one launch (start us, length us, event | category | flops | bytes accessed | tf_op | source)
XLA Modules:
  0.0 136.6 jit_solution(17590869444282698616)
XLA Ops:
  1.3 5.0 %collective-permute-start = (bf16[128,1024]{1,0:T(8,128)(2,1)}, bf16[128,1024]{1,0:T(8,128)(2,1)S(1)}, u32[]{:S(2)}, u32[]{:S(2)}) collective-permute-start(bf16[128,1024]{1,0:T(8,128)(2,1)} %param.10), channel_id=1, source_target_pairs={{0,0},{1,17},{2,34},{3,51},{4,68},{5,85},{6,102},{7,119},{8,8},{9,... | collective-permute-start | bytes 786440 | tf_op jit(solution)/shard_map/ppermute | solution.py:117
  7.0 8.0 %collective-permute-done.1 = bf16[128,1024]{1,0:T(8,128)(2,1)S(1)} collective-permute-done((bf16[128,1024]{1,0:T(8,128)(2,1)}, bf16[128,1024]{1,0:T(8,128)(2,1)S(1)}, u32[]{:S(2)}, u32[]{:S(2)}) %collective-permute-start.1) | collective-permute-done | bytes 262176 | tf_op jit(solution)/shard_map/ppermute | solution.py:124
  16.1 1.8 %broadcast_in_dim.5 = bf16[8,128,1024]{2,1,0:T(8,128)(2,1)} broadcast(bf16[128,1024]{1,0:T(8,128)(2,1)S(1)} %collective-permute-done), dimensions={1,2} | broadcast | bytes 2359296 | tf_op jit(solution)/shard_map/broadcast_in_dim | solution.py:133
  18.1 7.3 %all-to-all-start = ((bf16[8,128,1024]{2,1,0:T(8,128)(2,1)}), bf16[8,128,1024]{2,1,0:T(8,128)(2,1)S(1)}, u32[]{:S(2)}, u32[]{:S(2)}) async-start(bf16[8,128,1024]{2,1,0:T(8,128)(2,1)} %broadcast_in_dim.5), calls=%async_computation | async-start | bytes 4194304 | tf_op jit(solution)/shard_map/all_to_all | solution.py:134
  25.5 2.0 %collective-permute-start.6 = (bf16[2,128,1024]{2,1,0:T(8,128)(2,1)S(1)}, bf16[2,128,1024]{2,1,0:T(8,128)(2,1)S(1)}, u32[]{:S(2)}, u32[]{:S(2)}) collective-permute-start(bf16[2,128,1024]{2,1,0:T(8,128)(2,1)S(1)} %pad_maximum_fusion), channel_id=1, source_target_pairs={{0,96},{1,97},{2,98},{3,99},{4,100},{5,101},{6,102},{7,103},{8,104... | collective-permute-start | bytes 1572872 | tf_op jit(solution)/shard_map/ppermute | solution.py:129
  27.8 10.6 %collective-permute-done.5 = bf16[2,128,1024]{2,1,0:T(8,128)(2,1)S(1)} collective-permute-done((bf16[2,128,1024]{2,1,0:T(8,128)(2,1)S(1)}, bf16[2,128,1024]{2,1,0:T(8,128)(2,1)S(1)}, u32[]{:S(2)}, u32[]{:S(2)}) %collective-permute-start.5) | collective-permute-done | bytes 524320 | tf_op jit(solution)/shard_map/ppermute | solution.py:129
  38.5 1.6 %collective-permute-start.7 = (bf16[1,128,1024]{2,1,0:T(8,128)(2,1)S(1)}, bf16[1,128,1024]{2,1,0:T(8,128)(2,1)S(1)}, u32[]{:S(2)}, u32[]{:S(2)}) collective-permute-start(bf16[1,128,1024]{2,1,0:T(8,128)(2,1)S(1)} %slice.145), channel_id=1, source_target_pairs={{0,32},{1,33},{2,34},{3,35},{4,36},{5,37},{6,38},{7,39},{8,40},{9,... | collective-permute-start | bytes 786440 | tf_op jit(solution)/shard_map/ppermute | solution.py:130
  40.8 4.2 %collective-permute-done.7 = bf16[1,128,1024]{2,1,0:T(8,128)(2,1)S(1)} collective-permute-done((bf16[1,128,1024]{2,1,0:T(8,128)(2,1)S(1)}, bf16[1,128,1024]{2,1,0:T(8,128)(2,1)S(1)}, u32[]{:S(2)}, u32[]{:S(2)}) %collective-permute-start.7) | collective-permute-done | bytes 262176 | tf_op jit(solution)/shard_map/ppermute | solution.py:130
  45.0 2.7 %collective-permute-done.8 = bf16[1,128,1024]{2,1,0:T(8,128)(2,1)S(1)} collective-permute-done((bf16[1,128,1024]{2,1,0:T(8,128)(2,1)S(1)}, bf16[1,128,1024]{2,1,0:T(8,128)(2,1)S(1)}, u32[]{:S(2)}, u32[]{:S(2)}) %collective-permute-start.8) | collective-permute-done | bytes 262176 | tf_op jit(solution)/shard_map/ppermute | solution.py:130
  47.8 5.6 %shard_map.64 = bf16[8,128,1024]{2,1,0:T(8,128)(2,1)S(1)} custom-call(s32[9]{0:T(128)S(1)} %pad_add_fusion.1.place, bf16[8,128,1024]{2,1,0:T(8,128)(2,1)S(1)} %constant_dynamic-update-slice_fusion.part, f32[512,1024]{1,0:T(8,128)} %mine.7, f32[512,1024]{1,0:T(8,128)} %copy-done.2), custom_call_target="tpu_custom_call" | custom-call | flops 2147483648 | bytes 8388608 | tf_op jit(solution)/shard_map/pallas_call | solution.py:29
  54.2 1.5 %collective-permute-start.14 = (bf16[128,1024]{1,0:T(8,128)(2,1)}, bf16[128,1024]{1,0:T(8,128)(2,1)S(1)}, u32[]{:S(2)}, u32[]{:S(2)}) collective-permute-start(bf16[128,1024]{1,0:T(8,128)(2,1)} %get-tuple-element.54), channel_id=1, source_target_pairs={{0,1},{1,2},{2,3},{3,0},{4,5},{5,6},{6,7},{7,4},{8,9},{9,10},{10,1... | collective-permute-start | bytes 786440 | tf_op jit(solution)/shard_map/ppermute | solution.py:138
  55.7 1.8 %collective-permute-start.15 = (bf16[128,1024]{1,0:T(8,128)(2,1)S(1)}, bf16[128,1024]{1,0:T(8,128)(2,1)S(1)}, u32[]{:S(2)}, u32[]{:S(2)}) collective-permute-start(bf16[128,1024]{1,0:T(8,128)(2,1)S(1)} %get-tuple-element.53), channel_id=1, source_target_pairs={{0,3},{1,0},{2,1},{3,2},{4,7},{5,4},{6,5},{7,6},{8,11},{9,8},{10,9... | collective-permute-start | bytes 786440 | tf_op jit(solution)/shard_map/ppermute | solution.py:138
  57.5 5.1 %shard_map.65 = bf16[8,128,1024]{2,1,0:T(8,128)(2,1)S(1)} custom-call(s32[9]{0:T(128)S(1)} %pad_add_fusion.place, bf16[8,128,1024]{2,1,0:T(8,128)(2,1)S(1)} %all-to-all-done.part, f32[512,1024]{1,0:T(8,128)} %mine.5, f32[512,1024]{1,0:T(8,128)} %collective-permute-done.4.other), custom_call_target="tpu_custom_call" | custom-call | flops 2147483648 | bytes 8388608 | tf_op jit(solution)/shard_map/pallas_call | solution.py:29
  62.7 3.2 %collective-permute-start.9 = (bf16[128,1024]{1,0:T(8,128)(2,1)S(1)}, bf16[128,1024]{1,0:T(8,128)(2,1)S(1)}, u32[]{:S(2)}, u32[]{:S(2)}) collective-permute-start(bf16[128,1024]{1,0:T(8,128)(2,1)S(1)} %get-tuple-element.48), channel_id=1, source_target_pairs={{0,32},{1,33},{2,34},{3,35},{4,36},{5,37},{6,38},{7,39},{8,40},{9,... | collective-permute-start | bytes 786440 | tf_op jit(solution)/shard_map/ppermute | solution.py:138
  66.5 5.0 %shard_map.67 = bf16[8,128,1024]{2,1,0:T(8,128)(2,1)S(1)} custom-call(s32[9]{0:T(128)S(1)} %pad_add_fusion.2.place, bf16[8,128,1024]{2,1,0:T(8,128)(2,1)S(1)} %all-to-all-done.part, f32[512,1024]{1,0:T(8,128)} %mine.7, f32[512,1024]{1,0:T(8,128)} %copy-done.2), custom_call_target="tpu_custom_call" | custom-call | flops 2147483648 | bytes 8388608 | tf_op jit(solution)/shard_map/pallas_call | solution.py:29
  71.6 1.4 %collective-permute-start.16 = (bf16[4,128,1024]{2,1,0:T(8,128)(2,1)S(1)}, bf16[4,128,1024]{2,1,0:T(8,128)(2,1)S(1)}, u32[]{:S(2)}, u32[]{:S(2)}) collective-permute-start(bf16[4,128,1024]{2,1,0:T(8,128)(2,1)S(1)} %slice.154), channel_id=1, source_target_pairs={{0,16},{1,17},{2,18},{3,19},{4,20},{5,21},{6,22},{7,23},{8,24},{9,... | collective-permute-start | bytes 3145736 | tf_op jit(solution)/shard_map/ppermute | solution.py:165
  73.1 3.1 %collective-permute-start.20 = (bf16[2,128,1024]{2,1,0:T(8,128)(2,1)S(1)}, bf16[2,128,1024]{2,1,0:T(8,128)(2,1)S(1)}, u32[]{:S(2)}, u32[]{:S(2)}) collective-permute-start(bf16[2,128,1024]{2,1,0:T(8,128)(2,1)S(1)} %pad_maximum_fusion.4), channel_id=1, source_target_pairs={{0,3},{1,0},{2,1},{3,2},{4,7},{5,4},{6,5},{7,6},{8,11},{9,8},{10,9... | collective-permute-start | bytes 1572872 | tf_op jit(solution)/shard_map/ppermute | solution.py:155
  76.2 5.0 %shard_map.66 = bf16[8,128,1024]{2,1,0:T(8,128)(2,1)S(1)} custom-call(s32[9]{0:T(128)S(1)} %pad_add_fusion.place, bf16[8,128,1024]{2,1,0:T(8,128)(2,1)S(1)} %all-to-all-done.part, f32[512,1024]{1,0:T(8,128)} %mine.6, f32[512,1024]{1,0:T(8,128)} %collective-permute-done.2.other), custom_call_target="tpu_custom_call" | custom-call | flops 2147483648 | bytes 8388608 | tf_op jit(solution)/shard_map/pallas_call | solution.py:29
  81.3 2.0 %collective-permute-start.18 = (bf16[128,1024]{1,0:T(8,128)(2,1)S(1)}, bf16[128,1024]{1,0:T(8,128)(2,1)S(1)}, u32[]{:S(2)}, u32[]{:S(2)}) collective-permute-start(bf16[128,1024]{1,0:T(8,128)(2,1)S(1)} %get-tuple-element.55), channel_id=1, source_target_pairs={{0,96},{1,97},{2,98},{3,99},{4,100},{5,101},{6,102},{7,103},{8,104... | collective-permute-start | bytes 786440 | tf_op jit(solution)/shard_map/ppermute | solution.py:138
  83.8 3.2 %collective-permute-start.11 = (bf16[2,128,1024]{2,1,0:T(8,128)(2,1)S(1)}, bf16[2,128,1024]{2,1,0:T(8,128)(2,1)S(1)}, u32[]{:S(2)}, u32[]{:S(2)}) collective-permute-start(bf16[2,128,1024]{2,1,0:T(8,128)(2,1)S(1)} %pad_maximum_fusion.1), channel_id=1, source_target_pairs={{0,32},{1,33},{2,34},{3,35},{4,36},{5,37},{6,38},{7,39},{8,40},{9,... | collective-permute-start | bytes 1572872 | tf_op jit(solution)/shard_map/ppermute | solution.py:154
  87.3 3.2 %collective-permute-done.17 = bf16[128,1024]{1,0:T(8,128)(2,1)S(1)} collective-permute-done((bf16[128,1024]{1,0:T(8,128)(2,1)S(1)}, bf16[128,1024]{1,0:T(8,128)(2,1)S(1)}, u32[]{:S(2)}, u32[]{:S(2)}) %collective-permute-start.17) | collective-permute-done | bytes 262176 | tf_op jit(solution)/shard_map/ppermute | solution.py:138
  93.4 5.7 %collective-permute-done.12 = bf16[2,128,1024]{2,1,0:T(8,128)(2,1)S(1)} collective-permute-done((bf16[2,128,1024]{2,1,0:T(8,128)(2,1)S(1)}, bf16[2,128,1024]{2,1,0:T(8,128)(2,1)S(1)}, u32[]{:S(2)}, u32[]{:S(2)}) %collective-permute-start.12) | collective-permute-done | bytes 524320 | tf_op jit(solution)/shard_map/ppermute | solution.py:155
  99.1 1.8 %collective-permute-start.28 = (bf16[2,128,1024]{2,1,0:T(8,128)(2,1)S(1)}, bf16[2,128,1024]{2,1,0:T(8,128)(2,1)S(1)}, u32[]{:S(2)}, u32[]{:S(2)}) collective-permute-start(bf16[2,128,1024]{2,1,0:T(8,128)(2,1)S(1)} %pad_maximum_fusion.6), channel_id=1, source_target_pairs={{0,96},{1,97},{2,98},{3,99},{4,100},{5,101},{6,102},{7,103},{8,104... | collective-permute-start | bytes 1572872 | tf_op jit(solution)/shard_map/ppermute | solution.py:155
  102.9 4.1 %collective-permute-done.27 = bf16[2,128,1024]{2,1,0:T(8,128)(2,1)S(1)} collective-permute-done((bf16[2,128,1024]{2,1,0:T(8,128)(2,1)S(1)}, bf16[2,128,1024]{2,1,0:T(8,128)(2,1)S(1)}, u32[]{:S(2)}, u32[]{:S(2)}) %collective-permute-start.27) | collective-permute-done | bytes 524320 | tf_op jit(solution)/shard_map/ppermute | solution.py:154
  107.0 5.3 %collective-permute-done.28 = bf16[2,128,1024]{2,1,0:T(8,128)(2,1)S(1)} collective-permute-done((bf16[2,128,1024]{2,1,0:T(8,128)(2,1)S(1)}, bf16[2,128,1024]{2,1,0:T(8,128)(2,1)S(1)}, u32[]{:S(2)}, u32[]{:S(2)}) %collective-permute-start.28) | collective-permute-done | bytes 524320 | tf_op jit(solution)/shard_map/ppermute | solution.py:155
  113.0 1.9 %collective-permute-start.25 = (bf16[128,1024]{1,0:T(8,128)(2,1)S(1)}, bf16[128,1024]{1,0:T(8,128)(2,1)S(1)}, u32[]{:S(2)}, u32[]{:S(2)}) collective-permute-start(bf16[128,1024]{1,0:T(8,128)(2,1)S(1)} %bitcast_add_fusion.1), channel_id=1, source_target_pairs={{0,0},{1,17},{2,34},{3,51},{4,68},{5,85},{6,102},{7,119},{8,8},{9,... | collective-permute-start | bytes 786440 | tf_op jit(solution)/shard_map/ppermute | solution.py:201
  117.2 3.5 %collective-permute-start.23 = (bf16[128,1024]{1,0:T(8,128)(2,1)S(1)}, bf16[128,1024]{1,0:T(8,128)(2,1)S(1)}, u32[]{:S(2)}, u32[]{:S(2)}) collective-permute-start(bf16[128,1024]{1,0:T(8,128)(2,1)S(1)} %get-tuple-element.58), channel_id=1, source_target_pairs={{0,64},{1,65},{2,66},{3,67},{4,68},{5,69},{6,70},{7,71},{8,72},{9,... | collective-permute-start | bytes 786440 | tf_op jit(solution)/shard_map/ppermute | solution.py:159
  120.7 2.1 %collective-permute-done.25 = bf16[128,1024]{1,0:T(8,128)(2,1)S(1)} collective-permute-done((bf16[128,1024]{1,0:T(8,128)(2,1)S(1)}, bf16[128,1024]{1,0:T(8,128)(2,1)S(1)}, u32[]{:S(2)}, u32[]{:S(2)}) %collective-permute-start.25) | collective-permute-done | bytes 262176 | tf_op jit(solution)/shard_map/ppermute | solution.py:201
  122.8 1.9 %collective-permute-start.26 = (bf16[128,1024]{1,0:T(8,128)(2,1)S(1)}, bf16[128,1024]{1,0:T(8,128)(2,1)S(1)}, u32[]{:S(2)}, u32[]{:S(2)}) collective-permute-start(bf16[128,1024]{1,0:T(8,128)(2,1)S(1)} %collective-permute-done.25), channel_id=1, source_target_pairs={{0,0},{1,1},{2,2},{3,3},{4,4},{5,5},{6,6},{7,7},{8,8},{9,9},{10,10... | collective-permute-start | bytes 786440 | tf_op jit(solution)/shard_map/ppermute | solution.py:204
  125.6 2.8 %collective-permute-done.23 = bf16[128,1024]{1,0:T(8,128)(2,1)S(1)} collective-permute-done((bf16[128,1024]{1,0:T(8,128)(2,1)S(1)}, bf16[128,1024]{1,0:T(8,128)(2,1)S(1)}, u32[]{:S(2)}, u32[]{:S(2)}) %collective-permute-start.23) | collective-permute-done | bytes 262176 | tf_op jit(solution)/shard_map/ppermute | solution.py:159
  128.4 6.3 %collective-permute-done.26 = bf16[128,1024]{1,0:T(8,128)(2,1)S(1)} collective-permute-done((bf16[128,1024]{1,0:T(8,128)(2,1)S(1)}, bf16[128,1024]{1,0:T(8,128)(2,1)S(1)}, u32[]{:S(2)}, u32[]{:S(2)}) %collective-permute-start.26) | collective-permute-done | bytes 262176 | tf_op jit(solution)/shard_map/ppermute | solution.py:204
  134.9 1.7 %multiply_add_fusion = f32[4,128,1024]{2,1,0:T(8,128)} fusion(f32[128,1024]{1,0:T(8,128)S(1)} %bitcast_add_fusion, f32[4]{0:T(128)S(1)} %mul.49, f32[128,1024]{1,0:T(8,128)S(1)} %fusion.5, f32[4]{0:T(128)S(1)} %copy-done.3, f32[128,1024]{1,0:T(8,128)S(1)} %fusion.3), kind=kLoop, calls=%fused_computation | loop fusion | flops 2097152 | bytes 3670048 | tf_op jit(solution)/shard_map/add | solution.py:209
  (89 shorter events, 15.6 us)
Async XLA Ops:
  0.0 16.1 %collective-permute-start.3 = (f32[512,1024]{1,0:T(8,128)}, f32[512,1024]{1,0:T(8,128)S(1)}, u32[]{:S(2)}, u32[]{:S(2)}) collective-permute-start(f32[512,1024]{1,0:T(8,128)} %mine.7), channel_id=1, source_target_pairs={{0,8},{1,9},{2,10},{3,11},{4,12},{5,13},{6,14},{7,15},{8,0},{9,1},... | collective-permute-start | bytes 6291464 | tf_op jit(solution)/shard_map/ppermute | solution.py:126
  0.0 16.1 %collective-permute-start.2 = (f32[512,1024]{1,0:T(8,128)}, f32[512,1024]{1,0:T(8,128)}, u32[]{:S(2)}, u32[]{:S(2)}) collective-permute-start(f32[512,1024]{1,0:T(8,128)} %mine.6), channel_id=1, source_target_pairs={{0,8},{1,9},{2,10},{3,11},{4,12},{5,13},{6,14},{7,15},{8,0},{9,1},... | collective-permute-start | bytes 6291464 | tf_op jit(solution)/shard_map/ppermute | solution.py:126
  0.5 15.6 %collective-permute-start.4 = (f32[512,1024]{1,0:T(8,128)}, f32[512,1024]{1,0:T(8,128)}, u32[]{:S(2)}, u32[]{:S(2)}) collective-permute-start(f32[512,1024]{1,0:T(8,128)} %mine.5), channel_id=1, source_target_pairs={{0,8},{1,9},{2,10},{3,11},{4,12},{5,13},{6,14},{7,15},{8,0},{9,1},... | collective-permute-start | bytes 6291464 | tf_op jit(solution)/shard_map/ppermute | solution.py:126
  0.5 14.5 %collective-permute-start.1 = (bf16[128,1024]{1,0:T(8,128)(2,1)}, bf16[128,1024]{1,0:T(8,128)(2,1)S(1)}, u32[]{:S(2)}, u32[]{:S(2)}) collective-permute-start(bf16[128,1024]{1,0:T(8,128)(2,1)} %param.10), channel_id=1, source_target_pairs={{0,16},{1,17},{2,18},{3,19},{4,20},{5,21},{6,22},{7,23},{8,24},{9,... | collective-permute-start | bytes 786440 | tf_op jit(solution)/shard_map/ppermute | solution.py:124
  1.3 14.9 %collective-permute-start = (bf16[128,1024]{1,0:T(8,128)(2,1)}, bf16[128,1024]{1,0:T(8,128)(2,1)S(1)}, u32[]{:S(2)}, u32[]{:S(2)}) collective-permute-start(bf16[128,1024]{1,0:T(8,128)(2,1)} %param.10), channel_id=1, source_target_pairs={{0,0},{1,17},{2,34},{3,51},{4,68},{5,85},{6,102},{7,119},{8,8},{9,... | collective-permute-start | bytes 786440 | tf_op jit(solution)/shard_map/ppermute | solution.py:117
  18.1 39.4 %all-to-all-start = ((bf16[8,128,1024]{2,1,0:T(8,128)(2,1)}), bf16[8,128,1024]{2,1,0:T(8,128)(2,1)S(1)}, u32[]{:S(2)}, u32[]{:S(2)}) async-start(bf16[8,128,1024]{2,1,0:T(8,128)(2,1)} %broadcast_in_dim.5), calls=%async_computation | async-start | bytes 4194304 | tf_op jit(solution)/shard_map/all_to_all | solution.py:134
  25.4 13.1 %collective-permute-start.5 = (bf16[2,128,1024]{2,1,0:T(8,128)(2,1)S(1)}, bf16[2,128,1024]{2,1,0:T(8,128)(2,1)S(1)}, u32[]{:S(2)}, u32[]{:S(2)}) collective-permute-start(bf16[2,128,1024]{2,1,0:T(8,128)(2,1)S(1)} %pad_maximum_fusion), channel_id=1, source_target_pairs={{0,32},{1,33},{2,34},{3,35},{4,36},{5,37},{6,38},{7,39},{8,40},{9,... | collective-permute-start | bytes 1572872 | tf_op jit(solution)/shard_map/ppermute | solution.py:129
  25.5 14.5 %collective-permute-start.6 = (bf16[2,128,1024]{2,1,0:T(8,128)(2,1)S(1)}, bf16[2,128,1024]{2,1,0:T(8,128)(2,1)S(1)}, u32[]{:S(2)}, u32[]{:S(2)}) collective-permute-start(bf16[2,128,1024]{2,1,0:T(8,128)(2,1)S(1)} %pad_maximum_fusion), channel_id=1, source_target_pairs={{0,96},{1,97},{2,98},{3,99},{4,100},{5,101},{6,102},{7,103},{8,104... | collective-permute-start | bytes 1572872 | tf_op jit(solution)/shard_map/ppermute | solution.py:129
  38.5 6.5 %collective-permute-start.7 = (bf16[1,128,1024]{2,1,0:T(8,128)(2,1)S(1)}, bf16[1,128,1024]{2,1,0:T(8,128)(2,1)S(1)}, u32[]{:S(2)}, u32[]{:S(2)}) collective-permute-start(bf16[1,128,1024]{2,1,0:T(8,128)(2,1)S(1)} %slice.145), channel_id=1, source_target_pairs={{0,32},{1,33},{2,34},{3,35},{4,36},{5,37},{6,38},{7,39},{8,40},{9,... | collective-permute-start | bytes 786440 | tf_op jit(solution)/shard_map/ppermute | solution.py:130
  40.1 7.7 %collective-permute-start.8 = (bf16[1,128,1024]{2,1,0:T(8,128)(2,1)S(1)}, bf16[1,128,1024]{2,1,0:T(8,128)(2,1)S(1)}, u32[]{:S(2)}, u32[]{:S(2)}) collective-permute-start(bf16[1,128,1024]{2,1,0:T(8,128)(2,1)S(1)} %slice.146), channel_id=1, source_target_pairs={{0,96},{1,97},{2,98},{3,99},{4,100},{5,101},{6,102},{7,103},{8,104... | collective-permute-start | bytes 786440 | tf_op jit(solution)/shard_map/ppermute | solution.py:130
  54.2 11.7 %collective-permute-start.14 = (bf16[128,1024]{1,0:T(8,128)(2,1)}, bf16[128,1024]{1,0:T(8,128)(2,1)S(1)}, u32[]{:S(2)}, u32[]{:S(2)}) collective-permute-start(bf16[128,1024]{1,0:T(8,128)(2,1)} %get-tuple-element.54), channel_id=1, source_target_pairs={{0,1},{1,2},{2,3},{3,0},{4,5},{5,6},{6,7},{7,4},{8,9},{9,10},{10,1... | collective-permute-start | bytes 786440 | tf_op jit(solution)/shard_map/ppermute | solution.py:138
  55.7 10.3 %collective-permute-start.15 = (bf16[128,1024]{1,0:T(8,128)(2,1)S(1)}, bf16[128,1024]{1,0:T(8,128)(2,1)S(1)}, u32[]{:S(2)}, u32[]{:S(2)}) collective-permute-start(bf16[128,1024]{1,0:T(8,128)(2,1)S(1)} %get-tuple-element.53), channel_id=1, source_target_pairs={{0,3},{1,0},{2,1},{3,2},{4,7},{5,4},{6,5},{7,6},{8,11},{9,8},{10,9... | collective-permute-start | bytes 786440 | tf_op jit(solution)/shard_map/ppermute | solution.py:138
  62.6 18.6 %collective-permute-start.10 = (bf16[128,1024]{1,0:T(8,128)(2,1)S(1)}, bf16[128,1024]{1,0:T(8,128)(2,1)S(1)}, u32[]{:S(2)}, u32[]{:S(2)}) collective-permute-start(bf16[128,1024]{1,0:T(8,128)(2,1)S(1)} %get-tuple-element.47), channel_id=1, source_target_pairs={{0,96},{1,97},{2,98},{3,99},{4,100},{5,101},{6,102},{7,103},{8,104... | collective-permute-start | bytes 786440 | tf_op jit(solution)/shard_map/ppermute | solution.py:138
  62.7 18.6 %collective-permute-start.9 = (bf16[128,1024]{1,0:T(8,128)(2,1)S(1)}, bf16[128,1024]{1,0:T(8,128)(2,1)S(1)}, u32[]{:S(2)}, u32[]{:S(2)}) collective-permute-start(bf16[128,1024]{1,0:T(8,128)(2,1)S(1)} %get-tuple-element.48), channel_id=1, source_target_pairs={{0,32},{1,33},{2,34},{3,35},{4,36},{5,37},{6,38},{7,39},{8,40},{9,... | collective-permute-start | bytes 786440 | tf_op jit(solution)/shard_map/ppermute | solution.py:138
  66.3 17.4 %collective-permute-start.19 = (bf16[2,128,1024]{2,1,0:T(8,128)(2,1)S(1)}, bf16[2,128,1024]{2,1,0:T(8,128)(2,1)S(1)}, u32[]{:S(2)}, u32[]{:S(2)}) collective-permute-start(bf16[2,128,1024]{2,1,0:T(8,128)(2,1)S(1)} %pad_maximum_fusion.3), channel_id=1, source_target_pairs={{0,1},{1,2},{2,3},{3,0},{4,5},{5,6},{6,7},{7,4},{8,9},{9,10},{10,1... | collective-permute-start | bytes 1572872 | tf_op jit(solution)/shard_map/ppermute | solution.py:154
  71.6 41.0 %collective-permute-start.16 = (bf16[4,128,1024]{2,1,0:T(8,128)(2,1)S(1)}, bf16[4,128,1024]{2,1,0:T(8,128)(2,1)S(1)}, u32[]{:S(2)}, u32[]{:S(2)}) collective-permute-start(bf16[4,128,1024]{2,1,0:T(8,128)(2,1)S(1)} %slice.154), channel_id=1, source_target_pairs={{0,16},{1,17},{2,18},{3,19},{4,20},{5,21},{6,22},{7,23},{8,24},{9,... | collective-permute-start | bytes 3145736 | tf_op jit(solution)/shard_map/ppermute | solution.py:165
  73.1 10.7 %collective-permute-start.20 = (bf16[2,128,1024]{2,1,0:T(8,128)(2,1)S(1)}, bf16[2,128,1024]{2,1,0:T(8,128)(2,1)S(1)}, u32[]{:S(2)}, u32[]{:S(2)}) collective-permute-start(bf16[2,128,1024]{2,1,0:T(8,128)(2,1)S(1)} %pad_maximum_fusion.4), channel_id=1, source_target_pairs={{0,3},{1,0},{2,1},{3,2},{4,7},{5,4},{6,5},{7,6},{8,11},{9,8},{10,9... | collective-permute-start | bytes 1572872 | tf_op jit(solution)/shard_map/ppermute | solution.py:155
  81.2 9.3 %collective-permute-start.17 = (bf16[128,1024]{1,0:T(8,128)(2,1)S(1)}, bf16[128,1024]{1,0:T(8,128)(2,1)S(1)}, u32[]{:S(2)}, u32[]{:S(2)}) collective-permute-start(bf16[128,1024]{1,0:T(8,128)(2,1)S(1)} %get-tuple-element.56), channel_id=1, source_target_pairs={{0,32},{1,33},{2,34},{3,35},{4,36},{5,37},{6,38},{7,39},{8,40},{9,... | collective-permute-start | bytes 786440 | tf_op jit(solution)/shard_map/ppermute | solution.py:138
  81.3 10.1 %collective-permute-start.18 = (bf16[128,1024]{1,0:T(8,128)(2,1)S(1)}, bf16[128,1024]{1,0:T(8,128)(2,1)S(1)}, u32[]{:S(2)}, u32[]{:S(2)}) collective-permute-start(bf16[128,1024]{1,0:T(8,128)(2,1)S(1)} %get-tuple-element.55), channel_id=1, source_target_pairs={{0,96},{1,97},{2,98},{3,99},{4,100},{5,101},{6,102},{7,103},{8,104... | collective-permute-start | bytes 786440 | tf_op jit(solution)/shard_map/ppermute | solution.py:138
  83.7 15.4 %collective-permute-start.12 = (bf16[2,128,1024]{2,1,0:T(8,128)(2,1)S(1)}, bf16[2,128,1024]{2,1,0:T(8,128)(2,1)S(1)}, u32[]{:S(2)}, u32[]{:S(2)}) collective-permute-start(bf16[2,128,1024]{2,1,0:T(8,128)(2,1)S(1)} %pad_maximum_fusion.2), channel_id=1, source_target_pairs={{0,96},{1,97},{2,98},{3,99},{4,100},{5,101},{6,102},{7,103},{8,104... | collective-permute-start | bytes 1572872 | tf_op jit(solution)/shard_map/ppermute | solution.py:155
  83.8 17.6 %collective-permute-start.11 = (bf16[2,128,1024]{2,1,0:T(8,128)(2,1)S(1)}, bf16[2,128,1024]{2,1,0:T(8,128)(2,1)S(1)}, u32[]{:S(2)}, u32[]{:S(2)}) collective-permute-start(bf16[2,128,1024]{2,1,0:T(8,128)(2,1)S(1)} %pad_maximum_fusion.1), channel_id=1, source_target_pairs={{0,32},{1,33},{2,34},{3,35},{4,36},{5,37},{6,38},{7,39},{8,40},{9,... | collective-permute-start | bytes 1572872 | tf_op jit(solution)/shard_map/ppermute | solution.py:154
  91.5 11.4 %collective-permute-start.24 = (bf16[128,1024]{1,0:T(8,128)(2,1)S(1)}, bf16[128,1024]{1,0:T(8,128)(2,1)S(1)}, u32[]{:S(2)}, u32[]{:S(2)}) collective-permute-start(bf16[128,1024]{1,0:T(8,128)(2,1)S(1)} %fusion.18), channel_id=1, source_target_pairs={{0,4},{1,5},{2,6},{3,7},{4,0},{5,1},{6,2},{7,3},{8,12},{9,13},{10,... | collective-permute-start | bytes 786440 | tf_op jit(solution)/shard_map/ppermute | solution.py:165
  93.0 14.0 %collective-permute-start.27 = (bf16[2,128,1024]{2,1,0:T(8,128)(2,1)S(1)}, bf16[2,128,1024]{2,1,0:T(8,128)(2,1)S(1)}, u32[]{:S(2)}, u32[]{:S(2)}) collective-permute-start(bf16[2,128,1024]{2,1,0:T(8,128)(2,1)S(1)} %pad_maximum_fusion.5), channel_id=1, source_target_pairs={{0,32},{1,33},{2,34},{3,35},{4,36},{5,37},{6,38},{7,39},{8,40},{9,... | collective-permute-start | bytes 1572872 | tf_op jit(solution)/shard_map/ppermute | solution.py:154
  99.1 13.2 %collective-permute-start.28 = (bf16[2,128,1024]{2,1,0:T(8,128)(2,1)S(1)}, bf16[2,128,1024]{2,1,0:T(8,128)(2,1)S(1)}, u32[]{:S(2)}, u32[]{:S(2)}) collective-permute-start(bf16[2,128,1024]{2,1,0:T(8,128)(2,1)S(1)} %pad_maximum_fusion.6), channel_id=1, source_target_pairs={{0,96},{1,97},{2,98},{3,99},{4,100},{5,101},{6,102},{7,103},{8,104... | collective-permute-start | bytes 1572872 | tf_op jit(solution)/shard_map/ppermute | solution.py:155
  101.7 15.5 %collective-permute-start.13 = (bf16[128,1024]{1,0:T(8,128)(2,1)S(1)}, bf16[128,1024]{1,0:T(8,128)(2,1)S(1)}, u32[]{:S(2)}, u32[]{:S(2)}) collective-permute-start(bf16[128,1024]{1,0:T(8,128)(2,1)S(1)} %fusion.17), channel_id=1, source_target_pairs={{0,16},{1,17},{2,18},{3,19},{4,20},{5,21},{6,22},{7,23},{8,24},{9,... | collective-permute-start | bytes 786440 | tf_op jit(solution)/shard_map/ppermute | solution.py:165
  113.0 9.8 %collective-permute-start.25 = (bf16[128,1024]{1,0:T(8,128)(2,1)S(1)}, bf16[128,1024]{1,0:T(8,128)(2,1)S(1)}, u32[]{:S(2)}, u32[]{:S(2)}) collective-permute-start(bf16[128,1024]{1,0:T(8,128)(2,1)S(1)} %bitcast_add_fusion.1), channel_id=1, source_target_pairs={{0,0},{1,17},{2,34},{3,51},{4,68},{5,85},{6,102},{7,119},{8,8},{9,... | collective-permute-start | bytes 786440 | tf_op jit(solution)/shard_map/ppermute | solution.py:201
  114.9 9.8 %collective-permute-start.29 = (bf16[128,1024]{1,0:T(8,128)(2,1)S(1)}, bf16[128,1024]{1,0:T(8,128)(2,1)S(1)}, u32[]{:S(2)}, u32[]{:S(2)}) collective-permute-start(bf16[128,1024]{1,0:T(8,128)(2,1)S(1)} %fusion.19), channel_id=1, source_target_pairs={{0,16},{1,17},{2,18},{3,19},{4,20},{5,21},{6,22},{7,23},{8,24},{9,... | collective-permute-start | bytes 786440 | tf_op jit(solution)/shard_map/ppermute | solution.py:165
  115.1 9.8 %collective-permute-start.21 = (bf16[128,1024]{1,0:T(8,128)(2,1)S(1)}, bf16[128,1024]{1,0:T(8,128)(2,1)S(1)}, u32[]{:S(2)}, u32[]{:S(2)}) collective-permute-start(bf16[128,1024]{1,0:T(8,128)(2,1)S(1)} %get-tuple-element.57), channel_id=1, source_target_pairs={{0,32},{1,33},{2,34},{3,35},{4,36},{5,37},{6,38},{7,39},{8,40},{9,... | collective-permute-start | bytes 786440 | tf_op jit(solution)/shard_map/ppermute | solution.py:159
  116.3 9.3 %collective-permute-start.22 = (bf16[128,1024]{1,0:T(8,128)(2,1)S(1)}, bf16[128,1024]{1,0:T(8,128)(2,1)S(1)}, u32[]{:S(2)}, u32[]{:S(2)}) collective-permute-start(bf16[128,1024]{1,0:T(8,128)(2,1)S(1)} %get-tuple-element.59), channel_id=1, source_target_pairs={{0,96},{1,97},{2,98},{3,99},{4,100},{5,101},{6,102},{7,103},{8,104... | collective-permute-start | bytes 786440 | tf_op jit(solution)/shard_map/ppermute | solution.py:159
  117.2 17.7 %copy-start.3 = (f32[4]{0:T(128)S(1)}, f32[4]{0:T(128)}, u32[]{:S(2)}) copy-start(f32[4]{0:T(128)} %param.9) | copy-start | bytes 52
  117.2 11.2 %collective-permute-start.23 = (bf16[128,1024]{1,0:T(8,128)(2,1)S(1)}, bf16[128,1024]{1,0:T(8,128)(2,1)S(1)}, u32[]{:S(2)}, u32[]{:S(2)}) collective-permute-start(bf16[128,1024]{1,0:T(8,128)(2,1)S(1)} %get-tuple-element.58), channel_id=1, source_target_pairs={{0,64},{1,65},{2,66},{3,67},{4,68},{5,69},{6,70},{7,71},{8,72},{9,... | collective-permute-start | bytes 786440 | tf_op jit(solution)/shard_map/ppermute | solution.py:159
  122.8 11.9 %collective-permute-start.26 = (bf16[128,1024]{1,0:T(8,128)(2,1)S(1)}, bf16[128,1024]{1,0:T(8,128)(2,1)S(1)}, u32[]{:S(2)}, u32[]{:S(2)}) collective-permute-start(bf16[128,1024]{1,0:T(8,128)(2,1)S(1)} %collective-permute-done.25), channel_id=1, source_target_pairs={{0,0},{1,1},{2,2},{3,3},{4,4},{5,5},{6,6},{7,7},{8,8},{9,9},{10,10... | collective-permute-start | bytes 786440 | tf_op jit(solution)/shard_map/ppermute | solution.py:204
  (4 other events, 20.2 us)
where the time goes:
time: 137 us
  waiting for transfers between devices  57.2 us (42%)
  starting transfers between devices  48.7 us (36%)
  Pallas kernels  20.6 us (15%)
  other arithmetic  6.13 us (4%)
  local copies, waits for them, and re-layouts  3.38 us (2%)
    pallas_call x4, Pallas kernels, call(): pl.pallas_call(body, grid_spec=pltpu.PrefetchScalarGridSpec(num_scalar_pr...  20.6 us
    ppermute x3, waiting for transfers between devices, finish(): lax.ppermute(off, BOTH, back).astype(F32)  11 us
    ppermute x1, waiting for transfers between devices, shards(): lax.ppermute(pair, BOTH, z_ring[0])  10.6 us
    ppermute x1, waiting for transfers between devices, shards(): lax.ppermute(modes, BOTH, moves(n_row, n_col, lambda block, core, col: (b...  8.02 us
    all_to_all x1, starting transfers between devices, shards(): lax.all_to_all(copies, 'col', split_axis=0, concat_axis=0, tiled=True)  7.26 us
    ppermute x1, waiting for transfers between devices, shards(): lax.ppermute(home, BOTH, moves(n_row, n_col, lambda block, core, col: (bl...  6.29 us
    ppermute x3, starting transfers between devices, ring_sum(): lax.ppermute(parts[i], BOTH, pairs[i]).astype(F32)  5.61 us
    ppermute x3, starting transfers between devices, finish(): lax.ppermute(off, BOTH, back).astype(F32)  5.01 us
  transfers between devices with their start and end apart: 31, of which 14 were waited for; matrix products, arithmetic and copies ran while one was open for 4% of the time, Pallas kernels for 15%

commit v1 on v0

--- a/solution.py
+++ b/solution.py
@@ -187,9 +187,9 @@
     step_t = join(*later(step_t, product_y))
     product_a = untransposed(after(swath, step_t[1]), *cross_pair, here_y)
     product_a = product_a.reshape((2, 4) + product_a.shape[1:])
-    product_x = untransposed(after(swath, product_a), *gram_x_pair, here)
+    step_y = join(*later(step_y, product_a))
+    product_x = untransposed(after(swath, product_a, step_y[1]), *gram_x_pair, here)
     step_x = start(product_x, *z_ring)
-    step_y = join(*later(step_y, product_x))
     total_t = after(finish(step_t, *x_ring), step_y[1])
     step_x = join(*later(step_x, total_t))
     half_a = after(fold(product_a, y_near, BF16).astype(BF16), step_x[1])
@@ -197,10 +197,10 @@
     total_t = after(fold(total_t, y_far, BF16), half_a)
     from_gram_y = fold(finish(step_y, *z_ring), y_near, BF16)
     from_gram_x = fold(after(finish(step_x, *z_ring), total_t), y_near, BF16)
-    from_cross_t = ring_sum(half_a, z_turns)
     home = lax.ppermute(
         total_t.astype(BF16), BOTH, moves(n_row, n_col, lambda block, core, col: (block ^ col, core, col))
     )
+    from_cross_t = ring_sum(after(half_a, home), z_turns)
     home = lax.ppermute(home, BOTH, moves(n_row, n_col, lambda block, core, col: (block, core, col ^ block)))
     from_cross = home.astype(F32)
 

time: 137 us -> 135 us (0.985); the launches traced: 137 us -> 132 us
  waiting for transfers between devices: 57.2 us -> 47.9 us
  starting transfers between devices: 48.7 us -> 53.7 us
    ppermute x3, waiting for transfers between devices: 11 us -> 5.72 us  [finish(): lax.ppermute(off, BOTH, back).astype(F32)]
    ppermute x3, starting transfers between devices: 3.79 us -> 7.74 us  [finish(): lax.ppermute(on, BOTH, ahead).astype(F32)]
    ppermute x3, waiting for transfers between devices: 4.55 us -> 1.18 us  [finish(): lax.ppermute(on, BOTH, ahead).astype(F32)]
    ppermute x1, waiting for transfers between devices: 6.29 us -> 3.02 us  [shards(): lax.ppermute(home, BOTH, moves(n_row, n_col, lambda block, core, col: (bl...]
    ppermute x4, waiting for transfers between devices: 0.01 us -> 2.64 us  [fold(): lax.ppermute(total[1].astype(dtype), BOTH, partner).astype(F32)]
    ppermute x3, starting transfers between devices: 5.01 us -> 2.52 us  [finish(): lax.ppermute(off, BOTH, back).astype(F32)]
    ppermute x1, starting transfers between devices: 1.91 us -> 4.32 us  [shards(): lax.ppermute(home, BOTH, moves(n_row, n_col, lambda block, core, col: (bl...]
    ppermute x1, waiting for transfers between devices: 2.09 us -> 0.01 us  [shards(): lax.ppermute(total_t.astype(BF16), BOTH, moves(n_row, n_col, lambda block...]
  transfers between devices with their start and end apart: 31 -> 31, of which waited for: 14 -> 11; matrix products, arithmetic and copies ran while one was open for 4% -> 4% of each run, Pallas kernels for 15% -> 16%
where the time goes in v1:
time: 135 us; the launch traced here: 132 us
  starting transfers between devices  53.7 us (40%)
  waiting for transfers between devices  47.9 us (35%)
  Pallas kernels  20.6 us (15%)
  other arithmetic  6.92 us (5%)
  local copies, waits for them, and re-layouts  2.59 us (2%)
    pallas_call x4, Pallas kernels, call(): pl.pallas_call(body, grid_spec=pltpu.PrefetchScalarGridSpec(num_scalar_pr...  20.6 us
    ppermute x1, waiting for transfers between devices, shards(): lax.ppermute(pair, BOTH, z_ring[0])  10.7 us
    ppermute x1, waiting for transfers between devices, shards(): lax.ppermute(modes, BOTH, moves(n_row, n_col, lambda block, core, col: (b...  8.02 us
    ppermute x3, starting transfers between devices, finish(): lax.ppermute(on, BOTH, ahead).astype(F32)  7.74 us
    all_to_all x1, starting transfers between devices, shards(): lax.all_to_all(copies, 'col', split_axis=0, concat_axis=0, tiled=True)  7.26 us
    ppermute x3, waiting for transfers between devices, finish(): lax.ppermute(off, BOTH, back).astype(F32)  5.72 us
    ppermute x4, starting transfers between devices, fold(): lax.ppermute(total[1].astype(dtype), BOTH, partner).astype(F32)  5.6 us
    ppermute x3, waiting for transfers between devices, start(): lax.ppermute(parts[2, 0], BOTH, ahead)  5.03 us
  transfers between devices with their start and end apart: 31, of which 11 were waited for; matrix products, arithmetic and copies ran while one was open for 4% of the time, Pallas kernels for 16%

profile of v1, /device:TPU:120, one launch (start us, length us, event | category | flops | bytes accessed | tf_op | source)
XLA Modules:
  0.0 132.3 jit_solution(16185535309713002471)
XLA Ops:
  1.3 5.0 %collective-permute-start = (bf16[128,1024]{1,0:T(8,128)(2,1)}, bf16[128,1024]{1,0:T(8,128)(2,1)S(1)}, u32[]{:S(2)}, u32[]{:S(2)}) collective-permute-start(bf16[128,1024]{1,0:T(8,128)(2,1)} %param.10), channel_id=1, source_target_pairs={{0,0},{1,17},{2,34},{3,51},{4,68},{5,85},{6,102},{7,119},{8,8},{9,... | collective-permute-start | bytes 786440 | tf_op jit(solution)/shard_map/ppermute | solution.py:117
  7.0 8.0 %collective-permute-done.1 = bf16[128,1024]{1,0:T(8,128)(2,1)S(1)} collective-permute-done((bf16[128,1024]{1,0:T(8,128)(2,1)}, bf16[128,1024]{1,0:T(8,128)(2,1)S(1)}, u32[]{:S(2)}, u32[]{:S(2)}) %collective-permute-start.1) | collective-permute-done | bytes 262176 | tf_op jit(solution)/shard_map/ppermute | solution.py:124
  16.1 1.8 %broadcast_in_dim.5 = bf16[8,128,1024]{2,1,0:T(8,128)(2,1)} broadcast(bf16[128,1024]{1,0:T(8,128)(2,1)S(1)} %collective-permute-done), dimensions={1,2} | broadcast | bytes 2359296 | tf_op jit(solution)/shard_map/broadcast_in_dim | solution.py:133
  18.1 7.3 %all-to-all-start = ((bf16[8,128,1024]{2,1,0:T(8,128)(2,1)}), bf16[8,128,1024]{2,1,0:T(8,128)(2,1)S(1)}, u32[]{:S(2)}, u32[]{:S(2)}) async-start(bf16[8,128,1024]{2,1,0:T(8,128)(2,1)} %broadcast_in_dim.5), calls=%async_computation | async-start | bytes 4194304 | tf_op jit(solution)/shard_map/all_to_all | solution.py:134
  25.5 2.0 %collective-permute-start.6 = (bf16[2,128,1024]{2,1,0:T(8,128)(2,1)S(1)}, bf16[2,128,1024]{2,1,0:T(8,128)(2,1)S(1)}, u32[]{:S(2)}, u32[]{:S(2)}) collective-permute-start(bf16[2,128,1024]{2,1,0:T(8,128)(2,1)S(1)} %pad_maximum_fusion), channel_id=1, source_target_pairs={{0,96},{1,97},{2,98},{3,99},{4,100},{5,101},{6,102},{7,103},{8,104... | collective-permute-start | bytes 1572872 | tf_op jit(solution)/shard_map/ppermute | solution.py:129
  27.7 10.7 %collective-permute-done.5 = bf16[2,128,1024]{2,1,0:T(8,128)(2,1)S(1)} collective-permute-done((bf16[2,128,1024]{2,1,0:T(8,128)(2,1)S(1)}, bf16[2,128,1024]{2,1,0:T(8,128)(2,1)S(1)}, u32[]{:S(2)}, u32[]{:S(2)}) %collective-permute-start.5) | collective-permute-done | bytes 524320 | tf_op jit(solution)/shard_map/ppermute | solution.py:129
  38.5 1.6 %collective-permute-start.7 = (bf16[1,128,1024]{2,1,0:T(8,128)(2,1)S(1)}, bf16[1,128,1024]{2,1,0:T(8,128)(2,1)S(1)}, u32[]{:S(2)}, u32[]{:S(2)}) collective-permute-start(bf16[1,128,1024]{2,1,0:T(8,128)(2,1)S(1)} %slice.145), channel_id=1, source_target_pairs={{0,32},{1,33},{2,34},{3,35},{4,36},{5,37},{6,38},{7,39},{8,40},{9,... | collective-permute-start | bytes 786440 | tf_op jit(solution)/shard_map/ppermute | solution.py:130
  40.8 4.2 %collective-permute-done.7 = bf16[1,128,1024]{2,1,0:T(8,128)(2,1)S(1)} collective-permute-done((bf16[1,128,1024]{2,1,0:T(8,128)(2,1)S(1)}, bf16[1,128,1024]{2,1,0:T(8,128)(2,1)S(1)}, u32[]{:S(2)}, u32[]{:S(2)}) %collective-permute-start.7) | collective-permute-done | bytes 262176 | tf_op jit(solution)/shard_map/ppermute | solution.py:130
  45.0 2.7 %collective-permute-done.8 = bf16[1,128,1024]{2,1,0:T(8,128)(2,1)S(1)} collective-permute-done((bf16[1,128,1024]{2,1,0:T(8,128)(2,1)S(1)}, bf16[1,128,1024]{2,1,0:T(8,128)(2,1)S(1)}, u32[]{:S(2)}, u32[]{:S(2)}) %collective-permute-start.8) | collective-permute-done | bytes 262176 | tf_op jit(solution)/shard_map/ppermute | solution.py:130
  47.8 5.6 %shard_map.64 = bf16[8,128,1024]{2,1,0:T(8,128)(2,1)S(1)} custom-call(s32[9]{0:T(128)S(1)} %pad_add_fusion.1.place, bf16[8,128,1024]{2,1,0:T(8,128)(2,1)S(1)} %constant_dynamic-update-slice_fusion.part, f32[512,1024]{1,0:T(8,128)} %mine.6, f32[512,1024]{1,0:T(8,128)} %copy-done.2), custom_call_target="tpu_custom_call" | custom-call | flops 2147483648 | bytes 8388608 | tf_op jit(solution)/shard_map/pallas_call | solution.py:29
  53.4 1.5 %collective-permute-start.11 = (bf16[128,1024]{1,0:T(8,128)(2,1)S(1)}, bf16[128,1024]{1,0:T(8,128)(2,1)S(1)}, u32[]{:S(2)}, u32[]{:S(2)}) collective-permute-start(bf16[128,1024]{1,0:T(8,128)(2,1)S(1)} %get-tuple-element.60), channel_id=1, source_target_pairs={{0,1},{1,2},{2,3},{3,0},{4,5},{5,6},{6,7},{7,4},{8,9},{9,10},{10,1... | collective-permute-start | bytes 786440 | tf_op jit(solution)/shard_map/ppermute | solution.py:138
  55.0 1.8 %collective-permute-start.12 = (bf16[128,1024]{1,0:T(8,128)(2,1)S(1)}, bf16[128,1024]{1,0:T(8,128)(2,1)S(1)}, u32[]{:S(2)}, u32[]{:S(2)}) collective-permute-start(bf16[128,1024]{1,0:T(8,128)(2,1)S(1)} %get-tuple-element.59), channel_id=1, source_target_pairs={{0,3},{1,0},{2,1},{3,2},{4,7},{5,4},{6,5},{7,6},{8,11},{9,8},{10,9... | collective-permute-start | bytes 786440 | tf_op jit(solution)/shard_map/ppermute | solution.py:138
  56.8 5.1 %shard_map.65 = bf16[8,128,1024]{2,1,0:T(8,128)(2,1)S(1)} custom-call(s32[9]{0:T(128)S(1)} %pad_add_fusion.place, bf16[8,128,1024]{2,1,0:T(8,128)(2,1)S(1)} %all-to-all-done.part, f32[512,1024]{1,0:T(8,128)} %mine.5, f32[512,1024]{1,0:T(8,128)} %collective-permute-done.4.other), custom_call_target="tpu_custom_call" | custom-call | flops 2147483648 | bytes 8388608 | tf_op jit(solution)/shard_map/pallas_call | solution.py:29
  63.3 3.2 %collective-permute-start.9 = (bf16[128,1024]{1,0:T(8,128)(2,1)S(1)}, bf16[128,1024]{1,0:T(8,128)(2,1)S(1)}, u32[]{:S(2)}, u32[]{:S(2)}) collective-permute-start(bf16[128,1024]{1,0:T(8,128)(2,1)S(1)} %get-tuple-element.58), channel_id=1, source_target_pairs={{0,32},{1,33},{2,34},{3,35},{4,36},{5,37},{6,38},{7,39},{8,40},{9,... | collective-permute-start | bytes 786440 | tf_op jit(solution)/shard_map/ppermute | solution.py:138
  66.5 5.0 %shard_map.66 = bf16[8,128,1024]{2,1,0:T(8,128)(2,1)S(1)} custom-call(s32[9]{0:T(128)S(1)} %pad_add_fusion.2.place, bf16[8,128,1024]{2,1,0:T(8,128)(2,1)S(1)} %all-to-all-done.part, f32[512,1024]{1,0:T(8,128)} %mine.6, f32[512,1024]{1,0:T(8,128)} %copy-done.2), custom_call_target="tpu_custom_call" | custom-call | flops 2147483648 | bytes 8388608 | tf_op jit(solution)/shard_map/pallas_call | solution.py:29
  73.8 2.4 %collective-permute-start.20 = (bf16[2,128,1024]{2,1,0:T(8,128)(2,1)}, bf16[2,128,1024]{2,1,0:T(8,128)(2,1)S(1)}, u32[]{:S(2)}, u32[]{:S(2)}) collective-permute-start(bf16[2,128,1024]{2,1,0:T(8,128)(2,1)} %pad_maximum_fusion.4), channel_id=1, source_target_pairs={{0,3},{1,0},{2,1},{3,2},{4,7},{5,4},{6,5},{7,6},{8,11},{9,8},{10,9... | collective-permute-start | bytes 1572872 | tf_op jit(solution)/shard_map/ppermute | solution.py:155
  76.6 3.3 %collective-permute-start.13 = (bf16[2,128,1024]{2,1,0:T(8,128)(2,1)S(1)}, bf16[2,128,1024]{2,1,0:T(8,128)(2,1)S(1)}, u32[]{:S(2)}, u32[]{:S(2)}) collective-permute-start(bf16[2,128,1024]{2,1,0:T(8,128)(2,1)S(1)} %pad_maximum_fusion.2), channel_id=1, source_target_pairs={{0,32},{1,33},{2,34},{3,35},{4,36},{5,37},{6,38},{7,39},{8,40},{9,... | collective-permute-start | bytes 1572872 | tf_op jit(solution)/shard_map/ppermute | solution.py:154
  79.9 5.0 %shard_map.67 = bf16[8,128,1024]{2,1,0:T(8,128)(2,1)S(1)} custom-call(s32[9]{0:T(128)S(1)} %pad_add_fusion.place, bf16[8,128,1024]{2,1,0:T(8,128)(2,1)S(1)} %all-to-all-done.part, f32[512,1024]{1,0:T(8,128)} %mine.7, f32[512,1024]{1,0:T(8,128)} %collective-permute-done.2.other), custom_call_target="tpu_custom_call" | custom-call | flops 2147483648 | bytes 8388608 | tf_op jit(solution)/shard_map/pallas_call | solution.py:29
  85.1 2.0 %collective-permute-start.18 = (bf16[128,1024]{1,0:T(8,128)(2,1)S(1)}, bf16[128,1024]{1,0:T(8,128)(2,1)S(1)}, u32[]{:S(2)}, u32[]{:S(2)}) collective-permute-start(bf16[128,1024]{1,0:T(8,128)(2,1)S(1)} %get-tuple-element.55), channel_id=1, source_target_pairs={{0,96},{1,97},{2,98},{3,99},{4,100},{5,101},{6,102},{7,103},{8,104... | collective-permute-start | bytes 786440 | tf_op jit(solution)/shard_map/ppermute | solution.py:138
  87.4 5.0 %collective-permute-done.17 = bf16[128,1024]{1,0:T(8,128)(2,1)S(1)} collective-permute-done((bf16[128,1024]{1,0:T(8,128)(2,1)S(1)}, bf16[128,1024]{1,0:T(8,128)(2,1)S(1)}, u32[]{:S(2)}, u32[]{:S(2)}) %collective-permute-start.17) | collective-permute-done | bytes 262176 | tf_op jit(solution)/shard_map/ppermute | solution.py:138
  93.2 3.5 %collective-permute-start.27 = (bf16[2,128,1024]{2,1,0:T(8,128)(2,1)S(1)}, bf16[2,128,1024]{2,1,0:T(8,128)(2,1)S(1)}, u32[]{:S(2)}, u32[]{:S(2)}) collective-permute-start(bf16[2,128,1024]{2,1,0:T(8,128)(2,1)S(1)} %pad_maximum_fusion.5), channel_id=1, source_target_pairs={{0,32},{1,33},{2,34},{3,35},{4,36},{5,37},{6,38},{7,39},{8,40},{9,... | collective-permute-start | bytes 1572872 | tf_op jit(solution)/shard_map/ppermute | solution.py:154
  97.2 1.5 %collective-permute-start.15 = (bf16[128,1024]{1,0:T(8,128)(2,1)S(1)}, bf16[128,1024]{1,0:T(8,128)(2,1)S(1)}, u32[]{:S(2)}, u32[]{:S(2)}) collective-permute-start(bf16[128,1024]{1,0:T(8,128)(2,1)S(1)} %fusion.17), channel_id=1, source_target_pairs={{0,16},{1,17},{2,18},{3,19},{4,20},{5,21},{6,22},{7,23},{8,24},{9,... | collective-permute-start | bytes 786440 | tf_op jit(solution)/shard_map/ppermute | solution.py:165
  98.7 2.6 %collective-permute-done.21 = bf16[128,1024]{1,0:T(8,128)(2,1)S(1)} collective-permute-done((bf16[128,1024]{1,0:T(8,128)(2,1)S(1)}, bf16[128,1024]{1,0:T(8,128)(2,1)S(1)}, u32[]{:S(2)}, u32[]{:S(2)}) %collective-permute-start.21) | collective-permute-done | bytes 262176 | tf_op jit(solution)/shard_map/ppermute | solution.py:165
  101.8 3.2 %collective-permute-start.22 = (bf16[128,1024]{1,0:T(8,128)(2,1)S(1)}, bf16[128,1024]{1,0:T(8,128)(2,1)S(1)}, u32[]{:S(2)}, u32[]{:S(2)}) collective-permute-start(bf16[128,1024]{1,0:T(8,128)(2,1)S(1)} %bitcast_add_fusion.1), channel_id=1, source_target_pairs={{0,0},{1,17},{2,34},{3,51},{4,68},{5,85},{6,102},{7,119},{8,8},{9,... | collective-permute-start | bytes 786440 | tf_op jit(solution)/shard_map/ppermute | solution.py:200
  106.2 5.7 %collective-permute-done.28 = bf16[2,128,1024]{2,1,0:T(8,128)(2,1)S(1)} collective-permute-done((bf16[2,128,1024]{2,1,0:T(8,128)(2,1)S(1)}, bf16[2,128,1024]{2,1,0:T(8,128)(2,1)S(1)}, u32[]{:S(2)}, u32[]{:S(2)}) %collective-permute-start.28) | collective-permute-done | bytes 524320 | tf_op jit(solution)/shard_map/ppermute | solution.py:155
  112.2 2.4 %collective-permute-start.29 = (bf16[128,1024]{1,0:T(8,128)(2,1)S(1)}, bf16[128,1024]{1,0:T(8,128)(2,1)S(1)}, u32[]{:S(2)}, u32[]{:S(2)}) collective-permute-start(bf16[128,1024]{1,0:T(8,128)(2,1)S(1)} %fusion.19), channel_id=1, source_target_pairs={{0,16},{1,17},{2,18},{3,19},{4,20},{5,21},{6,22},{7,23},{8,24},{9,... | collective-permute-start | bytes 786440 | tf_op jit(solution)/shard_map/ppermute | solution.py:165
  114.7 2.2 %collective-permute-start.23 = (bf16[128,1024]{1,0:T(8,128)(2,1)S(1)}, bf16[128,1024]{1,0:T(8,128)(2,1)S(1)}, u32[]{:S(2)}, u32[]{:S(2)}) collective-permute-start(bf16[128,1024]{1,0:T(8,128)(2,1)S(1)} %get-tuple-element.61), channel_id=1, source_target_pairs={{0,32},{1,33},{2,34},{3,35},{4,36},{5,37},{6,38},{7,39},{8,40},{9,... | collective-permute-start | bytes 786440 | tf_op jit(solution)/shard_map/ppermute | solution.py:159
  117.0 1.5 %collective-permute-start.25 = (bf16[128,1024]{1,0:T(8,128)(2,1)S(1)}, bf16[128,1024]{1,0:T(8,128)(2,1)S(1)}, u32[]{:S(2)}, u32[]{:S(2)}) collective-permute-start(bf16[128,1024]{1,0:T(8,128)(2,1)S(1)} %get-tuple-element.62), channel_id=1, source_target_pairs={{0,64},{1,65},{2,66},{3,67},{4,68},{5,69},{6,70},{7,71},{8,72},{9,... | collective-permute-start | bytes 786440 | tf_op jit(solution)/shard_map/ppermute | solution.py:159
  118.5 4.3 %collective-permute-start.26 = (bf16[128,1024]{1,0:T(8,128)(2,1)S(1)}, bf16[128,1024]{1,0:T(8,128)(2,1)S(1)}, u32[]{:S(2)}, u32[]{:S(2)}) collective-permute-start(bf16[128,1024]{1,0:T(8,128)(2,1)S(1)} %collective-permute-done.22), channel_id=1, source_target_pairs={{0,0},{1,1},{2,2},{3,3},{4,4},{5,5},{6,6},{7,7},{8,8},{9,9},{10,10... | collective-permute-start | bytes 786440 | tf_op jit(solution)/shard_map/ppermute | solution.py:204
  123.0 4.4 %collective-permute-done.24 = bf16[128,1024]{1,0:T(8,128)(2,1)S(1)} collective-permute-done((bf16[128,1024]{1,0:T(8,128)(2,1)S(1)}, bf16[128,1024]{1,0:T(8,128)(2,1)S(1)}, u32[]{:S(2)}, u32[]{:S(2)}) %collective-permute-start.24) | collective-permute-done | bytes 262176 | tf_op jit(solution)/shard_map/ppermute | solution.py:159
  127.4 3.0 %collective-permute-done.26 = bf16[128,1024]{1,0:T(8,128)(2,1)S(1)} collective-permute-done((bf16[128,1024]{1,0:T(8,128)(2,1)S(1)}, bf16[128,1024]{1,0:T(8,128)(2,1)S(1)}, u32[]{:S(2)}, u32[]{:S(2)}) %collective-permute-start.26) | collective-permute-done | bytes 262176 | tf_op jit(solution)/shard_map/ppermute | solution.py:204
  130.6 1.7 %multiply_add_fusion = f32[4,128,1024]{2,1,0:T(8,128)} fusion(f32[128,1024]{1,0:T(8,128)S(1)} %bitcast_add_fusion, f32[4]{0:T(128)S(1)} %mul.49, f32[128,1024]{1,0:T(8,128)S(1)} %fusion.5, f32[4]{0:T(128)S(1)} %copy-done.3, f32[128,1024]{1,0:T(8,128)S(1)} %fusion.3), kind=kLoop, calls=%fused_computation | loop fusion | flops 2097152 | bytes 3670048 | tf_op jit(solution)/shard_map/add | solution.py:209
  (89 shorter events, 12.5 us)
Async XLA Ops:
  0.0 16.1 %collective-permute-start.3 = (f32[512,1024]{1,0:T(8,128)}, f32[512,1024]{1,0:T(8,128)S(1)}, u32[]{:S(2)}, u32[]{:S(2)}) collective-permute-start(f32[512,1024]{1,0:T(8,128)} %mine.6), channel_id=1, source_target_pairs={{0,8},{1,9},{2,10},{3,11},{4,12},{5,13},{6,14},{7,15},{8,0},{9,1},... | collective-permute-start | bytes 6291464 | tf_op jit(solution)/shard_map/ppermute | solution.py:126
  0.0 16.1 %collective-permute-start.2 = (f32[512,1024]{1,0:T(8,128)}, f32[512,1024]{1,0:T(8,128)}, u32[]{:S(2)}, u32[]{:S(2)}) collective-permute-start(f32[512,1024]{1,0:T(8,128)} %mine.7), channel_id=1, source_target_pairs={{0,8},{1,9},{2,10},{3,11},{4,12},{5,13},{6,14},{7,15},{8,0},{9,1},... | collective-permute-start | bytes 6291464 | tf_op jit(solution)/shard_map/ppermute | solution.py:126
  0.5 15.6 %collective-permute-start.4 = (f32[512,1024]{1,0:T(8,128)}, f32[512,1024]{1,0:T(8,128)}, u32[]{:S(2)}, u32[]{:S(2)}) collective-permute-start(f32[512,1024]{1,0:T(8,128)} %mine.5), channel_id=1, source_target_pairs={{0,8},{1,9},{2,10},{3,11},{4,12},{5,13},{6,14},{7,15},{8,0},{9,1},... | collective-permute-start | bytes 6291464 | tf_op jit(solution)/shard_map/ppermute | solution.py:126
  0.5 14.5 %collective-permute-start.1 = (bf16[128,1024]{1,0:T(8,128)(2,1)}, bf16[128,1024]{1,0:T(8,128)(2,1)S(1)}, u32[]{:S(2)}, u32[]{:S(2)}) collective-permute-start(bf16[128,1024]{1,0:T(8,128)(2,1)} %param.10), channel_id=1, source_target_pairs={{0,16},{1,17},{2,18},{3,19},{4,20},{5,21},{6,22},{7,23},{8,24},{9,... | collective-permute-start | bytes 786440 | tf_op jit(solution)/shard_map/ppermute | solution.py:124
  1.3 14.8 %collective-permute-start = (bf16[128,1024]{1,0:T(8,128)(2,1)}, bf16[128,1024]{1,0:T(8,128)(2,1)S(1)}, u32[]{:S(2)}, u32[]{:S(2)}) collective-permute-start(bf16[128,1024]{1,0:T(8,128)(2,1)} %param.10), channel_id=1, source_target_pairs={{0,0},{1,17},{2,34},{3,51},{4,68},{5,85},{6,102},{7,119},{8,8},{9,... | collective-permute-start | bytes 786440 | tf_op jit(solution)/shard_map/ppermute | solution.py:117
  18.1 38.7 %all-to-all-start = ((bf16[8,128,1024]{2,1,0:T(8,128)(2,1)}), bf16[8,128,1024]{2,1,0:T(8,128)(2,1)S(1)}, u32[]{:S(2)}, u32[]{:S(2)}) async-start(bf16[8,128,1024]{2,1,0:T(8,128)(2,1)} %broadcast_in_dim.5), calls=%async_computation | async-start | bytes 4194304 | tf_op jit(solution)/shard_map/all_to_all | solution.py:134
  25.4 13.1 %collective-permute-start.5 = (bf16[2,128,1024]{2,1,0:T(8,128)(2,1)S(1)}, bf16[2,128,1024]{2,1,0:T(8,128)(2,1)S(1)}, u32[]{:S(2)}, u32[]{:S(2)}) collective-permute-start(bf16[2,128,1024]{2,1,0:T(8,128)(2,1)S(1)} %pad_maximum_fusion), channel_id=1, source_target_pairs={{0,32},{1,33},{2,34},{3,35},{4,36},{5,37},{6,38},{7,39},{8,40},{9,... | collective-permute-start | bytes 1572872 | tf_op jit(solution)/shard_map/ppermute | solution.py:129
  25.5 14.5 %collective-permute-start.6 = (bf16[2,128,1024]{2,1,0:T(8,128)(2,1)S(1)}, bf16[2,128,1024]{2,1,0:T(8,128)(2,1)S(1)}, u32[]{:S(2)}, u32[]{:S(2)}) collective-permute-start(bf16[2,128,1024]{2,1,0:T(8,128)(2,1)S(1)} %pad_maximum_fusion), channel_id=1, source_target_pairs={{0,96},{1,97},{2,98},{3,99},{4,100},{5,101},{6,102},{7,103},{8,104... | collective-permute-start | bytes 1572872 | tf_op jit(solution)/shard_map/ppermute | solution.py:129
  38.5 6.5 %collective-permute-start.7 = (bf16[1,128,1024]{2,1,0:T(8,128)(2,1)S(1)}, bf16[1,128,1024]{2,1,0:T(8,128)(2,1)S(1)}, u32[]{:S(2)}, u32[]{:S(2)}) collective-permute-start(bf16[1,128,1024]{2,1,0:T(8,128)(2,1)S(1)} %slice.145), channel_id=1, source_target_pairs={{0,32},{1,33},{2,34},{3,35},{4,36},{5,37},{6,38},{7,39},{8,40},{9,... | collective-permute-start | bytes 786440 | tf_op jit(solution)/shard_map/ppermute | solution.py:130
  40.1 7.7 %collective-permute-start.8 = (bf16[1,128,1024]{2,1,0:T(8,128)(2,1)S(1)}, bf16[1,128,1024]{2,1,0:T(8,128)(2,1)S(1)}, u32[]{:S(2)}, u32[]{:S(2)}) collective-permute-start(bf16[1,128,1024]{2,1,0:T(8,128)(2,1)S(1)} %slice.146), channel_id=1, source_target_pairs={{0,96},{1,97},{2,98},{3,99},{4,100},{5,101},{6,102},{7,103},{8,104... | collective-permute-start | bytes 786440 | tf_op jit(solution)/shard_map/ppermute | solution.py:130
  53.4 8.5 %collective-permute-start.11 = (bf16[128,1024]{1,0:T(8,128)(2,1)S(1)}, bf16[128,1024]{1,0:T(8,128)(2,1)S(1)}, u32[]{:S(2)}, u32[]{:S(2)}) collective-permute-start(bf16[128,1024]{1,0:T(8,128)(2,1)S(1)} %get-tuple-element.60), channel_id=1, source_target_pairs={{0,1},{1,2},{2,3},{3,0},{4,5},{5,6},{6,7},{7,4},{8,9},{9,10},{10,1... | collective-permute-start | bytes 786440 | tf_op jit(solution)/shard_map/ppermute | solution.py:138
  55.0 6.9 %collective-permute-start.12 = (bf16[128,1024]{1,0:T(8,128)(2,1)S(1)}, bf16[128,1024]{1,0:T(8,128)(2,1)S(1)}, u32[]{:S(2)}, u32[]{:S(2)}) collective-permute-start(bf16[128,1024]{1,0:T(8,128)(2,1)S(1)} %get-tuple-element.59), channel_id=1, source_target_pairs={{0,3},{1,0},{2,1},{3,2},{4,7},{5,4},{6,5},{7,6},{8,11},{9,8},{10,9... | collective-permute-start | bytes 786440 | tf_op jit(solution)/shard_map/ppermute | solution.py:138
  62.2 22.9 %collective-permute-start.19 = (bf16[2,128,1024]{2,1,0:T(8,128)(2,1)S(1)}, bf16[2,128,1024]{2,1,0:T(8,128)(2,1)S(1)}, u32[]{:S(2)}, u32[]{:S(2)}) collective-permute-start(bf16[2,128,1024]{2,1,0:T(8,128)(2,1)S(1)} %pad_maximum_fusion.1), channel_id=1, source_target_pairs={{0,1},{1,2},{2,3},{3,0},{4,5},{5,6},{6,7},{7,4},{8,9},{9,10},{10,1... | collective-permute-start | bytes 1572872 | tf_op jit(solution)/shard_map/ppermute | solution.py:154
  63.2 13.0 %collective-permute-start.10 = (bf16[128,1024]{1,0:T(8,128)(2,1)S(1)}, bf16[128,1024]{1,0:T(8,128)(2,1)S(1)}, u32[]{:S(2)}, u32[]{:S(2)}) collective-permute-start(bf16[128,1024]{1,0:T(8,128)(2,1)S(1)} %get-tuple-element.57), channel_id=1, source_target_pairs={{0,96},{1,97},{2,98},{3,99},{4,100},{5,101},{6,102},{7,103},{8,104... | collective-permute-start | bytes 786440 | tf_op jit(solution)/shard_map/ppermute | solution.py:138
  63.3 12.9 %collective-permute-start.9 = (bf16[128,1024]{1,0:T(8,128)(2,1)S(1)}, bf16[128,1024]{1,0:T(8,128)(2,1)S(1)}, u32[]{:S(2)}, u32[]{:S(2)}) collective-permute-start(bf16[128,1024]{1,0:T(8,128)(2,1)S(1)} %get-tuple-element.58), channel_id=1, source_target_pairs={{0,32},{1,33},{2,34},{3,35},{4,36},{5,37},{6,38},{7,39},{8,40},{9,... | collective-permute-start | bytes 786440 | tf_op jit(solution)/shard_map/ppermute | solution.py:138
  71.6 29.8 %collective-permute-start.16 = (bf16[4,128,1024]{2,1,0:T(8,128)(2,1)S(1)}, bf16[4,128,1024]{2,1,0:T(8,128)(2,1)S(1)}, u32[]{:S(2)}, u32[]{:S(2)}) collective-permute-start(bf16[4,128,1024]{2,1,0:T(8,128)(2,1)S(1)} %slice.154), channel_id=1, source_target_pairs={{0,16},{1,17},{2,18},{3,19},{4,20},{5,21},{6,22},{7,23},{8,24},{9,... | collective-permute-start | bytes 3145736 | tf_op jit(solution)/shard_map/ppermute | solution.py:165
  73.8 11.2 %collective-permute-start.20 = (bf16[2,128,1024]{2,1,0:T(8,128)(2,1)}, bf16[2,128,1024]{2,1,0:T(8,128)(2,1)S(1)}, u32[]{:S(2)}, u32[]{:S(2)}) collective-permute-start(bf16[2,128,1024]{2,1,0:T(8,128)(2,1)} %pad_maximum_fusion.4), channel_id=1, source_target_pairs={{0,3},{1,0},{2,1},{3,2},{4,7},{5,4},{6,5},{7,6},{8,11},{9,8},{10,9... | collective-permute-start | bytes 1572872 | tf_op jit(solution)/shard_map/ppermute | solution.py:155
  76.5 20.3 %collective-permute-start.14 = (bf16[2,128,1024]{2,1,0:T(8,128)(2,1)S(1)}, bf16[2,128,1024]{2,1,0:T(8,128)(2,1)S(1)}, u32[]{:S(2)}, u32[]{:S(2)}) collective-permute-start(bf16[2,128,1024]{2,1,0:T(8,128)(2,1)S(1)} %pad_maximum_fusion.3), channel_id=1, source_target_pairs={{0,96},{1,97},{2,98},{3,99},{4,100},{5,101},{6,102},{7,103},{8,104... | collective-permute-start | bytes 1572872 | tf_op jit(solution)/shard_map/ppermute | solution.py:155
  76.6 20.2 %collective-permute-start.13 = (bf16[2,128,1024]{2,1,0:T(8,128)(2,1)S(1)}, bf16[2,128,1024]{2,1,0:T(8,128)(2,1)S(1)}, u32[]{:S(2)}, u32[]{:S(2)}) collective-permute-start(bf16[2,128,1024]{2,1,0:T(8,128)(2,1)S(1)} %pad_maximum_fusion.2), channel_id=1, source_target_pairs={{0,32},{1,33},{2,34},{3,35},{4,36},{5,37},{6,38},{7,39},{8,40},{9,... | collective-permute-start | bytes 1572872 | tf_op jit(solution)/shard_map/ppermute | solution.py:154
  85.0 7.4 %collective-permute-start.17 = (bf16[128,1024]{1,0:T(8,128)(2,1)S(1)}, bf16[128,1024]{1,0:T(8,128)(2,1)S(1)}, u32[]{:S(2)}, u32[]{:S(2)}) collective-permute-start(bf16[128,1024]{1,0:T(8,128)(2,1)S(1)} %get-tuple-element.56), channel_id=1, source_target_pairs={{0,32},{1,33},{2,34},{3,35},{4,36},{5,37},{6,38},{7,39},{8,40},{9,... | collective-permute-start | bytes 786440 | tf_op jit(solution)/shard_map/ppermute | solution.py:138
  85.1 7.8 %collective-permute-start.18 = (bf16[128,1024]{1,0:T(8,128)(2,1)S(1)}, bf16[128,1024]{1,0:T(8,128)(2,1)S(1)}, u32[]{:S(2)}, u32[]{:S(2)}) collective-permute-start(bf16[128,1024]{1,0:T(8,128)(2,1)S(1)} %get-tuple-element.55), channel_id=1, source_target_pairs={{0,96},{1,97},{2,98},{3,99},{4,100},{5,101},{6,102},{7,103},{8,104... | collective-permute-start | bytes 786440 | tf_op jit(solution)/shard_map/ppermute | solution.py:138
  92.4 8.9 %collective-permute-start.21 = (bf16[128,1024]{1,0:T(8,128)(2,1)S(1)}, bf16[128,1024]{1,0:T(8,128)(2,1)S(1)}, u32[]{:S(2)}, u32[]{:S(2)}) collective-permute-start(bf16[128,1024]{1,0:T(8,128)(2,1)S(1)} %fusion.18), channel_id=1, source_target_pairs={{0,4},{1,5},{2,6},{3,7},{4,0},{5,1},{6,2},{7,3},{8,12},{9,13},{10,... | collective-permute-start | bytes 786440 | tf_op jit(solution)/shard_map/ppermute | solution.py:165
  93.2 13.0 %collective-permute-start.27 = (bf16[2,128,1024]{2,1,0:T(8,128)(2,1)S(1)}, bf16[2,128,1024]{2,1,0:T(8,128)(2,1)S(1)}, u32[]{:S(2)}, u32[]{:S(2)}) collective-permute-start(bf16[2,128,1024]{2,1,0:T(8,128)(2,1)S(1)} %pad_maximum_fusion.5), channel_id=1, source_target_pairs={{0,32},{1,33},{2,34},{3,35},{4,36},{5,37},{6,38},{7,39},{8,40},{9,... | collective-permute-start | bytes 1572872 | tf_op jit(solution)/shard_map/ppermute | solution.py:154
  96.8 15.2 %collective-permute-start.28 = (bf16[2,128,1024]{2,1,0:T(8,128)(2,1)S(1)}, bf16[2,128,1024]{2,1,0:T(8,128)(2,1)S(1)}, u32[]{:S(2)}, u32[]{:S(2)}) collective-permute-start(bf16[2,128,1024]{2,1,0:T(8,128)(2,1)S(1)} %pad_maximum_fusion.6), channel_id=1, source_target_pairs={{0,96},{1,97},{2,98},{3,99},{4,100},{5,101},{6,102},{7,103},{8,104... | collective-permute-start | bytes 1572872 | tf_op jit(solution)/shard_map/ppermute | solution.py:155
  97.2 21.4 %collective-permute-start.15 = (bf16[128,1024]{1,0:T(8,128)(2,1)S(1)}, bf16[128,1024]{1,0:T(8,128)(2,1)S(1)}, u32[]{:S(2)}, u32[]{:S(2)}) collective-permute-start(bf16[128,1024]{1,0:T(8,128)(2,1)S(1)} %fusion.17), channel_id=1, source_target_pairs={{0,16},{1,17},{2,18},{3,19},{4,20},{5,21},{6,22},{7,23},{8,24},{9,... | collective-permute-start | bytes 786440 | tf_op jit(solution)/shard_map/ppermute | solution.py:165
  101.8 12.9 %collective-permute-start.22 = (bf16[128,1024]{1,0:T(8,128)(2,1)S(1)}, bf16[128,1024]{1,0:T(8,128)(2,1)S(1)}, u32[]{:S(2)}, u32[]{:S(2)}) collective-permute-start(bf16[128,1024]{1,0:T(8,128)(2,1)S(1)} %bitcast_add_fusion.1), channel_id=1, source_target_pairs={{0,0},{1,17},{2,34},{3,51},{4,68},{5,85},{6,102},{7,119},{8,8},{9,... | collective-permute-start | bytes 786440 | tf_op jit(solution)/shard_map/ppermute | solution.py:200
  112.2 10.7 %collective-permute-start.29 = (bf16[128,1024]{1,0:T(8,128)(2,1)S(1)}, bf16[128,1024]{1,0:T(8,128)(2,1)S(1)}, u32[]{:S(2)}, u32[]{:S(2)}) collective-permute-start(bf16[128,1024]{1,0:T(8,128)(2,1)S(1)} %fusion.19), channel_id=1, source_target_pairs={{0,16},{1,17},{2,18},{3,19},{4,20},{5,21},{6,22},{7,23},{8,24},{9,... | collective-permute-start | bytes 786440 | tf_op jit(solution)/shard_map/ppermute | solution.py:165
  114.7 8.3 %collective-permute-start.23 = (bf16[128,1024]{1,0:T(8,128)(2,1)S(1)}, bf16[128,1024]{1,0:T(8,128)(2,1)S(1)}, u32[]{:S(2)}, u32[]{:S(2)}) collective-permute-start(bf16[128,1024]{1,0:T(8,128)(2,1)S(1)} %get-tuple-element.61), channel_id=1, source_target_pairs={{0,32},{1,33},{2,34},{3,35},{4,36},{5,37},{6,38},{7,39},{8,40},{9,... | collective-permute-start | bytes 786440 | tf_op jit(solution)/shard_map/ppermute | solution.py:159
  117.0 10.4 %collective-permute-start.24 = (bf16[128,1024]{1,0:T(8,128)(2,1)S(1)}, bf16[128,1024]{1,0:T(8,128)(2,1)S(1)}, u32[]{:S(2)}, u32[]{:S(2)}) collective-permute-start(bf16[128,1024]{1,0:T(8,128)(2,1)S(1)} %get-tuple-element.63), channel_id=1, source_target_pairs={{0,96},{1,97},{2,98},{3,99},{4,100},{5,101},{6,102},{7,103},{8,104... | collective-permute-start | bytes 786440 | tf_op jit(solution)/shard_map/ppermute | solution.py:159
  117.0 13.6 %copy-start.3 = (f32[4]{0:T(128)S(1)}, f32[4]{0:T(128)}, u32[]{:S(2)}) copy-start(f32[4]{0:T(128)} %param.9) | copy-start | bytes 52
  117.0 10.4 %collective-permute-start.25 = (bf16[128,1024]{1,0:T(8,128)(2,1)S(1)}, bf16[128,1024]{1,0:T(8,128)(2,1)S(1)}, u32[]{:S(2)}, u32[]{:S(2)}) collective-permute-start(bf16[128,1024]{1,0:T(8,128)(2,1)S(1)} %get-tuple-element.62), channel_id=1, source_target_pairs={{0,64},{1,65},{2,66},{3,67},{4,68},{5,69},{6,70},{7,71},{8,72},{9,... | collective-permute-start | bytes 786440 | tf_op jit(solution)/shard_map/ppermute | solution.py:159
  118.5 11.9 %collective-permute-start.26 = (bf16[128,1024]{1,0:T(8,128)(2,1)S(1)}, bf16[128,1024]{1,0:T(8,128)(2,1)S(1)}, u32[]{:S(2)}, u32[]{:S(2)}) collective-permute-start(bf16[128,1024]{1,0:T(8,128)(2,1)S(1)} %collective-permute-done.22), channel_id=1, source_target_pairs={{0,0},{1,1},{2,2},{3,3},{4,4},{5,5},{6,6},{7,7},{8,8},{9,9},{10,10... | collective-permute-start | bytes 786440 | tf_op jit(solution)/shard_map/ppermute | solution.py:204
  (4 other events, 20.1 us)
